TPU v7x, 256 devices: a whole 4x4x8 slice. The times are simulated.
256 devices in a mesh: prow: 16 (over z_lo, x), pcol: 16 (over z_hi, y, core).
Axes of the slice: x: 4, y: 4, z: 8 (z_hi: 2, z_lo: 4; z = z_hi * 4 + z_lo), core: 2. Of those that a mesh axis runs over, the one named last changes fastest.
Arguments:
- features: bfloat16 [65536, 1024], P('prow', 'pcol'), may hold values from -6 to 6
- panel_offsets: int32 [2], replicated, may hold values from 0 to 480, as said below
- length_scale: float32 [1], replicated, may hold values from 30 to 60
- variance: float32 [1], replicated, may hold values from 0.5 to 2
Outputs:
- panels: float32 [2, 65536, 4096], P(None, 'prow', 'pcol')
Inputs may be any that keep to these rules, and one draw needn't show every extreme that they name: panel_offsets[1] is 480 and panel_offsets[0] is smaller; a panel stays inside the matrix.
All inputs are finite; a program needn't handle non-finite values.
Results may differ from a plain program's by a relative error of at most 0.0003.
Values may be sent and summed in bfloat16 or wider, within the bound.
A program may use at most 128 MiB of HBM per device.

v0:
```python
import jax
import jax.numpy as jnp
from jax import lax
from jax.sharding import PartitionSpec as P

TB = 128
PT = 32


def matern(sq_dist, length_scale, variance):
    scaled = 5.0 * sq_dist / (length_scale[0] * length_scale[0])
    dist_a = jnp.sqrt(scaled)
    return variance[0] * (1.0 + dist_a + scaled / 3.0) * jnp.exp(-dist_a)


def select_tiles(piece, wanted, shape_out):
    valid = (wanted >= 0) & (wanted < piece.shape[0])
    safe = jnp.clip(wanted, 0, piece.shape[0] - 1).reshape(-1)
    taken = jnp.take(piece, safe, axis=0).reshape(shape_out)
    return jnp.where(valid[..., None], taken, jnp.zeros((), piece.dtype))


def on_device(features, panel_offsets, length_scale, variance):
    col_count = lax.axis_size("pcol")
    row_count = lax.axis_size("prow")
    rows_dev = features.shape[0]
    slice_width = features.shape[1]
    per_col = PT // col_count
    which_col = jnp.arange(col_count, dtype=jnp.int32)[:, None, None]
    which_panel = jnp.arange(2, dtype=jnp.int32)[None, :, None]
    which_step = jnp.arange(per_col, dtype=jnp.int32)[None, None, :]
    global_tile = panel_offsets[which_panel] + which_step * col_count + which_col
    owner = global_tile % row_count
    slot = global_tile // row_count
    first_row = owner * rows_dev + slot * TB
    wanted = first_row[..., None] + jnp.arange(TB, dtype=jnp.int32)
    shape_out = (col_count, 2, per_col, TB, slice_width)
    buffer = select_tiles(lax.all_gather(features, "prow", axis=0, tiled=True), wanted, shape_out)
    dealt = lax.all_to_all(buffer, "pcol", split_axis=0, concat_axis=4, tiled=True)
    col_width = 2 * per_col * TB
    columns = dealt.reshape(col_width, dealt.shape[4])
    col_norm = jnp.sum(jnp.square(columns.astype(jnp.float32)), axis=1)
    row_full = lax.all_gather(features, "pcol", axis=1, tiled=True)
    gram = lax.dot_general(
        row_full, columns, (((1,), (1,)), ((), ())), preferred_element_type=jnp.float32
    )
    row_norm = jnp.sum(jnp.square(row_full.astype(jnp.float32)), axis=1)
    sq_dist = jnp.maximum(row_norm[:, None] + col_norm[None, :] - 2.0 * gram, 0.0)
    kernel = matern(sq_dist, length_scale, variance)
    return kernel.reshape(rows_dev, 2, per_col * TB).transpose(1, 0, 2)


def solution(mesh):
    return jax.shard_map(
        on_device,
        mesh=mesh,
        in_specs=(P("prow", "pcol"), P(), P(), P()),
        out_specs=P(None, "prow", "pcol"),
        check_vma=False,
    )
```

profile of v0, /device:TPU:1, one launch (start us, length us, event | category | flops | bytes accessed | tf_op | source)
XLA Modules:
  0.0 363.8 jit_solution(9220395785780754501)
XLA Ops:
  6.5 0.0 copy-start
  6.5 0.0 all-gather.5.cloned.1.call-start
  6.5 2.4 copy.7
  8.9 0.0 all-gather.5.cloned.1.call-update
  8.9 0.0 all-gather.3.cloned.1.call-start
  9.0 0.7 all-gather.3.cloned.1.call-update
  9.7 0.0 copy-done
  9.7 0.6 gather_fusion
  10.4 0.1 broadcast_add_fusion
  10.4 0.1 fusion.5
  10.5 0.2 compare_and_fusion
  10.7 0.1 fusion.3
  10.8 188.8 %all-gather.5.cloned.1.call-done = bf16[65536,64]{1,0:T(8,128)(2,1)} async-done(((bf16[4096,64]{1,0:T(8,128)(2,1)}), bf16[65536,64]{1,0:T(8,128)(2,1)}) %all-gather.5.cloned.1.call-update) | async-done | bytes 8388624 | tf_op jit(solution)/shard_map/all_gather | solution.py:38
  199.7 29.8 %gather_fusion.1 = bf16[8192,64]{1,0:T(8,128)(2,1)S(1)} fusion(bf16[65536,64]{1,0:T(8,128)(2,1)} %all-gather.5.cloned.1.call-done, s32[8192]{0:T(1024)S(1)} %broadcast_clamp_fusion), kind=kCustom, calls=%fused_computation.1 | custom fusion | bytes 2129920 | tf_op jit(solution)/shard_map/jit(_take)/gather | solution.py:19
  229.5 1.1 copy.8
  230.6 2.0 broadcast_select_fusion.1
  232.6 7.5 %all-to-all-start = ((bf16[16,2,2,128,64]{3,2,1,4,0:T(2,128)(2,1)}), bf16[16,2,2,128,64]{3,2,1,4,0:T(2,128)(2,1)S(1)}, u32[]{:S(2)}, u32[]{:S(2)}) async-start(bf16[16,2,2,128,64]{3,2,1,4,0:T(2,128)(2,1)} %broadcast_select_fusion.1), calls=%async_computation | async-start | bytes 2097152 | tf_op jit(solution)/shard_map/all_to_all | solution.py:39
  241.4 84.9 %all-gather.3.cloned.1.call-done = bf16[4096,1024]{0,1:T(8,128)(2,1)} async-done(((bf16[4096,64]{0,1:T(8,128)(2,1)}), bf16[4096,1024]{0,1:T(8,128)(2,1)}) %all-gather.3.cloned.1.call-update) | async-done | bytes 8388624 | tf_op jit(solution)/shard_map/all_gather | solution.py:43
  326.3 5.1 %multiply_reduce_fusion = f32[4096]{0:T(1024)S(1)} fusion(bf16[4096,1024]{0,1:T(8,128)(2,1)} %all-gather.3.cloned.1.call-done), kind=kLoop, calls=%fused_computation.2 | loop fusion | flops 12578816 | bytes 8404992 | tf_op jit(solution)/shard_map/reduce_sum | solution.py:47
  331.4 0.0 all-to-all-done
  331.4 0.4 reshape.138
  331.8 1.1 multiply_reduce_fusion.1
  332.9 15.1 %exponential_multiply_fusion = f32[4096,512]{0,1:T(8,128)} fusion(bf16[512,1024]{0,1:T(8,128)(2,1)S(1)} %reshape.138, bf16[4096,1024]{0,1:T(8,128)(2,1)} %all-gather.3.cloned.1.call-done, f32[]{:T(128)} %bitcast.9, f32[512]{0:T(512)S(1)} %bitcast.32, f32[4096]{0:T(1024)S(1)} %multiply_reduce_fusion, f32[]{:T(128)} %bitcast.26), kind=kOutput, calls=%fused_computation.7 | convolution fusion | flops 4320133120 | bytes 17844232 | tf_op jit(solution)/shard_map/dot_general | solution.py:44
  348.1 8.9 %copy.9 = f32[4096,2,256]{2,0,1:T(8,128)} copy(f32[4096,2,256]{0,2,1:T(8,128)} %bitcast.29) | data formatting | bytes 16777216 | tf_op jit(solution)/shard_map/reshape | solution.py:50
  (5 shorter events, 0.1 us)
Async XLA Ops:
  6.5 3.2 copy-start
  6.5 193.1 %all-gather.5.cloned.1.call-start = ((), (), s32[]{:S(2)}) async-start(), calls=%async_computation.2 | async-start | bytes 17825792 | tf_op jit(solution)/shard_map/all_gather | solution.py:38
  8.9 317.4 %all-gather.3.cloned.1.call-start = ((), (), s32[]{:S(2)}) async-start(), calls=%async_computation.1 | async-start | bytes 8912896 | tf_op jit(solution)/shard_map/all_gather | solution.py:43
  232.6 98.7 %all-to-all-start = ((bf16[16,2,2,128,64]{3,2,1,4,0:T(2,128)(2,1)}), bf16[16,2,2,128,64]{3,2,1,4,0:T(2,128)(2,1)S(1)}, u32[]{:S(2)}, u32[]{:S(2)}) async-start(bf16[16,2,2,128,64]{3,2,1,4,0:T(2,128)(2,1)} %broadcast_select_fusion.1), calls=%async_computation | async-start | bytes 2097152 | tf_op jit(solution)/shard_map/all_to_all | solution.py:39
Sparse Core Ops, SparseCore 0:
  9.1 190.4 all-gather.4
  202.4 123.8 all-gather.2
where the time goes:
time: 364 us
  waiting for transfers between devices  274 us (75%)
  local copies, waits for them, and re-layouts  43.3 us (12%)
  matrix products  15.1 us (4%)
  between operations  14.8 us (4%)
  other arithmetic  8.67 us (2%)
  starting transfers between devices  7.5 us (2%)
    all_gather x1, waiting for transfers between devices, on_device(): lax.all_gather(features, 'prow', axis=0, tiled=True)  189 us
    all_gather x1, waiting for transfers between devices, on_device(): row_full = lax.all_gather(features, 'pcol', axis=1, tiled=True)  84.9 us
    gather x2, local copies, waits for them, and re-layouts, select_tiles(): taken = jnp.take(piece, safe, axis=0).reshape(shape_out)  30.9 us
    dot_general x1, matrix products, on_device(): lax.dot_general(row_full, columns, (((1,), (1,)), ((), ())), preferred_el...  15.1 us
    reshape x1, local copies, waits for them, and re-layouts, on_device(): return kernel.reshape(rows_dev, 2, per_col * TB).transpose(1, 0, 2)  8.89 us
    all_to_all x1, starting transfers between devices, on_device(): lax.all_to_all(buffer, 'pcol', split_axis=0, concat_axis=4, tiled=True)  7.45 us
  transfers between devices with their start and end apart: 3, of which 2 were waited for; matrix products, arithmetic and copies ran while one was open for 11% of the time, Pallas kernels for 0%

commit v1 on v0

v1 whole, which is shorter than its diff:
```python
import functools

import jax
import jax.numpy as jnp
from jax import lax
from jax.experimental import pallas as pl
from jax.experimental.pallas import tpu as pltpu
from jax.sharding import PartitionSpec as P

TB = 128
NC = 8
LOG2E = 1.4426950408889634
MESH = pl.DeviceIdType.MESH
BF16 = jnp.bfloat16
F32 = jnp.float32


def pick(options, which):
    which = jnp.full(options[0].shape, which, jnp.int32)
    out = options[0].astype(F32)
    for n, option in enumerate(options[1:], 1):
        out = jnp.where(which == n, option.astype(F32), out)
    return out.astype(BF16)


def kernel(off_ref, ls_ref, var_ref, x_hbm, o_ref, xv, tr, rows, cols, rot1, rot2, mine, cnorm,
           in_sem, s_sw, r_sw, s_row, r_row, s_sib, r_sib, s_rot, r_rot, s_tp, r_tp, s_cz, r_cz, s_cx, r_cx):
    r = lax.axis_index("prow")
    q = lax.axis_index("pcol")
    x = r % 4
    zl = r // 4
    c = q % 2
    oc = 1 - c
    y = (q // 2) % 4
    zh = q // 8
    rc = rows.shape[3]
    hc = rc // 2
    half = NC * rc

    def at_q(zhi, yy, cc):
        return {"prow": r, "pcol": zhi * 8 + yy * 2 + cc}

    def at_r(rr):
        return {"prow": rr, "pcol": q}

    sib = at_q(zh, y, oc)
    up = at_q(zh, (y + 1) % 4, c)
    down = at_q(zh, (y + 3) % 4, c)
    across = at_q(1 - zh, y, c)
    flip = {"prow": q, "pcol": r}

    load = pltpu.make_async_copy(x_hbm, xv, in_sem)
    load.start()
    bar = pltpu.get_barrier_semaphore()
    for d in (sib, up, down, across):
        pl.semaphore_signal(bar, inc=1, device_id=d, device_id_type=MESH)
    for d in range(1, 16):
        pl.semaphore_signal(bar, inc=1, device_id=at_r((r + d) % 16), device_id_type=MESH)

    @pl.when(q != r)
    def _():
        pl.semaphore_signal(bar, inc=1, device_id=flip, device_id_type=MESH)

    load.wait()
    off0 = off_ref[0]
    slot = lax.shift_right_logical(off0 - r + 15, 4)
    rot1[0] = pick([xv[:, s * TB:(s + 2) * TB] for s in range(xv.shape[1] // TB - 1)], slot)
    mine[1] = xv[:, xv.shape[1] - 2 * TB:]
    pl.semaphore_wait(bar, 19 + (q != r).astype(jnp.int32))

    def swap(i):
        return pltpu.make_async_remote_copy(
            xv.at[:, pl.ds(pl.multiple_of(oc * half + i * rc, rc), rc)], tr.at[i, c],
            s_sw.at[i], r_sw.at[i], device_id=sib, device_id_type=MESH)

    @pl.loop(0, NC)
    def _(i):
        swap(i).start()

    def turn(stage, d):
        buf = rot1 if stage == 0 else rot2
        step = 1 if stage == 0 else 4
        return pltpu.make_async_remote_copy(
            buf.at[0], buf.at[d], s_rot.at[stage, d - 1], r_rot.at[stage, d - 1],
            device_id=at_r((r + 16 - step * d) % 16), device_id_type=MESH)

    def flipped(p):
        return pltpu.make_async_remote_copy(
            mine.at[p], cols.at[p, zh * 2 + y // 2, (y % 2) * 2 + c], s_tp.at[p], r_tp.at[p],
            device_id=flip, device_id_type=MESH)

    def flip_start(p):
        @pl.when(q != r)
        def _():
            flipped(p).start()

        @pl.when(q == r)
        def _():
            cols[p, zl, x] = mine[p]

    def flip_wait(p):
        @pl.when(q != r)
        def _():
            flipped(p).wait_recv()

    def col_z(p, d):
        return pltpu.make_async_remote_copy(
            cols.at[p, zl, x], cols.at[p, zl, x], s_cz.at[p, d - 1], r_cz.at[p, d - 1],
            device_id=at_r((r + 4 * d) % 16), device_id_type=MESH)

    def col_z_wait(p, d):
        src = cols.at[p, (zl + 4 - d) % 4, x]
        return pltpu.make_async_remote_copy(
            src, src, s_cz.at[p, d - 1], r_cz.at[p, d - 1],
            device_id=at_r((r + 4 * d) % 16), device_id_type=MESH)

    def col_x(p, d):
        return pltpu.make_async_remote_copy(
            cols.at[p, :, x], cols.at[p, :, x], s_cx.at[p, d - 1], r_cx.at[p, d - 1],
            device_id=at_r(zl * 4 + (x + d) % 4), device_id_type=MESH)

    def col_x_wait(p, d):
        src = cols.at[p, :, (x + 4 - d) % 4]
        return pltpu.make_async_remote_copy(
            src, src, s_cx.at[p, d - 1], r_cx.at[p, d - 1],
            device_id=at_r(zl * 4 + (x + d) % 4), device_id_type=MESH)

    for d in (1, 2, 3):
        turn(0, d).start()
    flip_start(1)

    UP, DOWN, FUP, FDOWN, ACROSS = 0, 1, 2, 3, 8

    def base(g):
        return (zh if g == 0 else 1 - zh) * 4

    def row_copy(kind, i, block, lo, n, to):
        ref = rows.at[c, i, block, pl.ds(lo, n)]
        return pltpu.make_async_remote_copy(ref, ref, s_row.at[kind, i], r_row.at[kind, i],
                                            device_id=to, device_id_type=MESH)

    def send_up(g, i):
        return row_copy(4 * g + UP, i, base(g) + y, 0, rc, up)

    def send_down(g, i):
        return row_copy(4 * g + DOWN, i, base(g) + y, 0, rc, down)

    def send_across(i):
        return row_copy(ACROSS, i, base(0) + y, 0, rc, across)

    def pass_up(g, i):
        return row_copy(4 * g + FUP, i, base(g) + (y + 3) % 4, 0, hc, up)

    def pass_down(g, i):
        return row_copy(4 * g + FDOWN, i, base(g) + (y + 1) % 4, hc, hc, down)

    def got_up(g, i):
        return row_copy(4 * g + UP, i, base(g) + (y + 3) % 4, 0, rc, up)

    def got_down(g, i):
        return row_copy(4 * g + DOWN, i, base(g) + (y + 1) % 4, 0, rc, down)

    def got_across(i):
        return row_copy(ACROSS, i, base(1) + y, 0, rc, across)

    def got_pass_up(g, i):
        return row_copy(4 * g + FUP, i, base(g) + (y + 2) % 4, 0, hc, up)

    def got_pass_down(g, i):
        return row_copy(4 * g + FDOWN, i, base(g) + (y + 2) % 4, hc, hc, down)

    def share(g, i, h):
        ref = rows.at[h, i, pl.ds(base(g), 4)]
        return pltpu.make_async_remote_copy(ref, ref, s_sib.at[g, i], r_sib.at[g, i],
                                            device_id=sib, device_id_type=MESH)

    own = zh * 4 + y

    @pl.loop(0, NC)
    def _(i):
        tr[i, c] = xv[:, pl.ds(pl.multiple_of(c * half + i * rc, rc), rc)]
        pltpu.make_async_remote_copy(tr.at[i, oc], tr.at[i, oc], s_sw.at[i], r_sw.at[i],
                                     device_id=sib, device_id_type=MESH).wait_recv()
        rows[c, i, own] = tr[i].reshape(2 * tr.shape[2], rc).T
        send_across(i).start()
        send_up(0, i).start()
        send_down(0, i).start()

    for d in (1, 2, 3):
        turn(0, d).wait_recv()
    rot2[0] = pick([rot1[d] for d in range(4)], lax.bitwise_and(off0, 3))
    for d in (1, 2, 3):
        turn(1, d).start()

    def columns(step):
        if step == 0:
            flip_wait(1)
            for d in (1, 2, 3):
                col_z(1, d).start()
            for d in (1, 2, 3):
                turn(1, d).wait_recv()
            mine[0] = pick([rot2[d] for d in range(4)], lax.bitwise_and(lax.shift_right_logical(off0, 2), 3))
            flip_start(0)
        if step == 1:
            for d in (1, 2, 3):
                col_z_wait(1, d).wait_recv()
            for d in (1, 2, 3):
                col_x(1, d).start()
        if step == 2:
            flip_wait(0)
            for d in (1, 2, 3):
                col_z(0, d).start()
        if step == 3:
            for d in (1, 2, 3):
                col_z_wait(0, d).wait_recv()
            for d in (1, 2, 3):
                col_x(0, d).start()

    def stage_a(i):
        got_across(i).wait_recv()
        send_up(1, i).start()
        send_down(1, i).start()
        got_up(0, i).wait_recv()
        pass_up(0, i).start()
        got_down(0, i).wait_recv()
        pass_down(0, i).start()

    def stage_b(i):
        got_up(1, i).wait_recv()
        pass_up(1, i).start()
        got_down(1, i).wait_recv()
        pass_down(1, i).start()
        got_pass_up(0, i).wait_recv()
        got_pass_down(0, i).wait_recv()
        share(0, i, c).start()

    def stage_c(i):
        got_pass_up(1, i).wait_recv()
        got_pass_down(1, i).wait_recv()
        share(1, i, c).start()

    ls = ls_ref[0]
    var = var_ref[0]
    scale = 5.0 / (ls * ls)

    def norms():
        for p in (0, 1):
            for d in (1, 2, 3):
                col_x_wait(p, d).wait_recv()
            total = jnp.zeros((1, 2 * TB), F32)
            for a in range(4):
                for b in range(4):
                    total += jnp.sum(jnp.square(cols[p, a, b].astype(F32)), axis=0, keepdims=True)
            cnorm[p] = total

    def compute(h, i):
        lhs = jnp.concatenate([rows[h, i, k] for k in range(8)], axis=1)
        rn = jnp.sum(jnp.square(lhs.astype(F32)), axis=1, keepdims=True)
        for p in (0, 1):
            rhs = cols[p].reshape(lhs.shape[1], 2 * TB)
            gram = jnp.dot(lhs, rhs, preferred_element_type=F32)
            sq = jnp.maximum((rn + cnorm[p] - 2.0 * gram) * scale, 1e-30)
            dist = sq * lax.rsqrt(sq)
            out = (var * (1.0 + dist + sq * (1.0 / 3.0))) * jnp.exp2(dist * (-LOG2E))
            o_ref[p, pl.ds(pl.multiple_of(h * half + i * rc, rc), rc), :] = out

    def stage_d(i):
        share(0, i, oc).wait_recv()
        share(1, i, oc).wait_recv()

        @pl.loop(0, 2)
        def _(h):
            compute(h, i)

    LB, LC, LD = 4, 5, 6
    for i in range(4):
        columns(i)
        stage_a(i)

    @pl.loop(4, 5)
    def _(i):
        stage_a(i)
        stage_b(i - LB)

    @pl.loop(5, 6)
    def _(i):
        stage_a(i)
        stage_b(i - LB)
        stage_c(i - LC)

    norms()

    @pl.loop(6, NC)
    def _(i):
        stage_a(i)
        stage_b(i - LB)
        stage_c(i - LC)
        stage_d(i - LD)

    @pl.loop(NC, NC + 4)
    def _(i):
        stage_b(i - LB)
        stage_c(i - LC)
        stage_d(i - LD)

    @pl.loop(NC + 4, NC + 5)
    def _(i):
        stage_c(i - LC)
        stage_d(i - LD)

    @pl.loop(NC + 5, NC + 6)
    def _(i):
        stage_d(i - LD)

    for stage in (0, 1):
        for d in (1, 2, 3):
            turn(stage, d).wait_send()
    for p in (0, 1):
        @pl.when(q != r)
        def _():
            flipped(p).wait_send()

        for d in (1, 2, 3):
            col_z(p, d).wait_send()
            col_x(p, d).wait_send()

    @pl.loop(0, NC)
    def _(i):
        swap(i).wait_send()
        send_across(i).wait_send()
        for g in (0, 1):
            send_up(g, i).wait_send()
            send_down(g, i).wait_send()
            pass_up(g, i).wait_send()
            pass_down(g, i).wait_send()
            share(g, i, c).wait_send()


def on_device(features, panel_offsets, length_scale, variance):
    pts, width = features.shape
    rc = pts // (2 * NC)
    smem = pl.BlockSpec(memory_space=pltpu.SMEM)
    dma = pltpu.SemaphoreType.DMA
    return pl.pallas_call(
        kernel,
        out_shape=pltpu.VMEM((2, pts, 2 * TB), F32),
        in_specs=[smem, smem, smem, pl.BlockSpec(memory_space=pl.ANY)],
        out_specs=pl.BlockSpec(memory_space=pltpu.VMEM),
        scratch_shapes=[
            pltpu.VMEM((width, pts), BF16),
            pltpu.VMEM((NC, 2, width, rc), BF16),
            pltpu.VMEM((2, NC, 8, rc, 2 * width), BF16),
            pltpu.VMEM((2, 4, 4, width, 2 * TB), BF16),
            pltpu.VMEM((4, width, 2 * TB), BF16),
            pltpu.VMEM((4, width, 2 * TB), BF16),
            pltpu.VMEM((2, width, 2 * TB), BF16),
            pltpu.VMEM((2, 1, 2 * TB), F32),
            dma, dma((NC,)), dma((NC,)), dma((9, NC)), dma((9, NC)), dma((2, NC)), dma((2, NC)),
            dma((2, 3)), dma((2, 3)), dma((2,)), dma((2,)), dma((2, 3)), dma((2, 3)), dma((2, 3)), dma((2, 3)),
        ],
        compiler_params=pltpu.CompilerParams(
            collective_id=0, has_side_effects=True, vmem_limit_bytes=48 * 2**20),
        cost_estimate=pl.CostEstimate(flops=2 * pts * 1024 * 512, bytes_accessed=9 * 2**20, transcendentals=0),
        name="panels",
    )(panel_offsets, length_scale, variance, features.T)


def solution(mesh):
    return jax.shard_map(
        on_device,
        mesh=mesh,
        in_specs=(P("prow", "pcol"), P(), P(), P()),
        out_specs=P(None, "prow", "pcol"),
        check_vma=False,
    )
```

time: 364 us -> 88 us (0.24)
  waiting for transfers between devices: 274 us -> 0 us
  Pallas kernels: 0 us -> 83.2 us
  local copies, waits for them, and re-layouts: 43.3 us -> 3.4 us
  matrix products: 15.1 us -> 0 us
  between operations: 14.8 us -> 1.3 us
  other arithmetic: 8.67 us -> 0 us
  starting transfers between devices: 7.5 us -> 0 us
    all_gather x2 -> x0, waiting for transfers between devices: 274 us -> none  [the longest x1 189 us: on_device(): lax.all_gather(features, 'prow', axis=0, tiled=True)]
    pallas_call x0 -> x1, Pallas kernels: none -> 83.2 us  [on_device(): pl.pallas_call(kernel, out_shape=pltpu.VMEM((2, pts, 2 * TB), F32), in_sp...]
    gather x3 -> x0, local copies, waits for them, and re-layouts: 31.5 us -> none  [the longest x2 30.9 us: select_tiles(): taken = jnp.take(piece, safe, axis=0).reshape(shape_out)]
    dot_general x1 -> x0, matrix products: 15.1 us -> none  [on_device(): lax.dot_general(row_full, columns, (((1,), (1,)), ((), ())), preferred_el...]
    reshape x2 -> x0, local copies, waits for them, and re-layouts: 9.33 us -> none  [the longest x1 8.89 us: on_device(): return kernel.reshape(rows_dev, 2, per_col * TB).transpose(1, 0, 2)]
    all_to_all x1 -> x0, starting transfers between devices: 7.45 us -> none  [on_device(): lax.all_to_all(buffer, 'pcol', split_axis=0, concat_axis=4, tiled=True)]
    reduce_sum x2 -> x0, other arithmetic: 6.21 us -> none  [the longest x1 5.07 us: on_device(): row_norm = jnp.sum(jnp.square(row_full.astype(jnp.float32)), axis=1)]
  transfers between devices with their start and end apart: 3 -> 0, of which waited for: 2 -> 0; matrix products, arithmetic and copies ran while one was open for 11% -> 0% of each run, Pallas kernels for 0% -> 0%
where the time goes in v1:
time: 88 us; the launch traced here: 87.9 us
  Pallas kernels  83.2 us (95%)
  local copies, waits for them, and re-layouts  3.4 us (4%)
  between operations  1.3 us (1%)
    pallas_call x1, Pallas kernels, on_device(): pl.pallas_call(kernel, out_shape=pltpu.VMEM((2, pts, 2 * TB), F32), in_sp...  83.2 us
    unnamed x1, local copies, waits for them, and re-layouts  3.4 us

profile of v1, /device:TPU:1, one launch (start us, length us, event | category | flops | bytes accessed | tf_op | source)
XLA Modules:
  0.0 87.9 jit_solution(1039257800436899020)
XLA Ops:
  1.3 83.2 %panels.1 = f32[2,4096,256]{2,1,0:T(8,128)S(1)} custom-call(s32[2]{0:T(128)} %off_ref.1, f32[1]{0:T(128)S(6)} %copy.7.ls_ref, f32[1]{0:T(128)S(6)} %copy.8.var_ref, bf16[64,4096]{1,0:T(8,128)(2,1)} %bitcast.1), custom_call_target="tpu_custom_call" | custom-call | flops 4294967296 | bytes 9437184 | tf_op jit(solution)/shard_map/panels/pallas_call | solution.py:344
  84.5 3.4 %copy.6 = f32[2,4096,256]{2,1,0:T(8,128)} copy(f32[2,4096,256]{2,1,0:T(8,128)S(1)} %panels.1) | data formatting | bytes 16777216

commit v2 on v1

v2 whole, which is shorter than its diff:
```python
import functools

import jax
import jax.numpy as jnp
from jax import lax
from jax.experimental import pallas as pl
from jax.experimental.pallas import tpu as pltpu
from jax.sharding import PartitionSpec as P

TB = 128
NC = 8
AHEAD = 8
LAG = (2, 3, 4, 5)
ZWIN = 3
EARLY = (-1, 0)
OWN = (3, 3, 6, 8)
STEPS = (2, 4, 7)
CS1 = 7
LOG2E = 1.4426950408889634
MESH = pl.DeviceIdType.MESH
BF16 = jnp.bfloat16
F32 = jnp.float32


def pick(options, which):
    which = jnp.full(options[0].shape, which, jnp.int32)
    out = options[0].astype(F32)
    for n, option in enumerate(options[1:], 1):
        out = jnp.where(which == n, option.astype(F32), out)
    return out.astype(BF16)


def gathered(rows, i):
    return jnp.concatenate([
        jnp.concatenate([rows[h, i, k] for k in range(8)], axis=1) for h in (0, 1)], axis=0)


def col_norm(cols, p):
    total = jnp.zeros((1, 2 * TB), F32)
    for a in range(4):
        for b in range(4):
            total += jnp.sum(jnp.square(cols[p, a, b].astype(F32)), axis=0, keepdims=True)
    return total


def values(lhs, rn, columns, cn, scale, var):
    gram = jnp.dot(lhs, columns.reshape(lhs.shape[1], 2 * TB), preferred_element_type=F32)
    sq = jnp.maximum((rn + cn - 2.0 * gram) * scale, 1e-30)
    dist = sq * lax.rsqrt(sq)
    return (var * (1.0 + dist + sq * (1.0 / 3.0))) * jnp.exp2(dist * (-LOG2E))


def finish(ls_ref, var_ref, first, rows, cols, rnorm, o_hbm, stage, sem1, sem0):
    rc = rows.shape[3]
    half = NC * rc
    send = pltpu.make_async_copy(first, o_hbm.at[1], sem1)
    send.start()
    ls = ls_ref[0]
    var = var_ref[0]
    scale = 5.0 / (ls * ls)
    cn = col_norm(cols, 0)

    def out_copy(i, h):
        at = pl.ds(pl.multiple_of(h * half + i * rc, rc), rc)
        return pltpu.make_async_copy(stage.at[at], o_hbm.at[0, at], sem0.at[i, h])

    @pl.loop(0, NC)
    def _(i):
        out = values(gathered(rows, i), rnorm[i], cols[0], cn, scale, var)
        for h in (0, 1):
            stage[pl.ds(pl.multiple_of(h * half + i * rc, rc), rc), :] = out[h * rc:(h + 1) * rc]
            out_copy(i, h).start()

    send.wait()

    @pl.loop(0, NC)
    def _(i):
        for h in (0, 1):
            out_copy(i, h).wait()


def kernel(off_ref, ls_ref, var_ref, x_hbm, o_ref, rows, cols, rnorm, xv, tr, rot1, rot2, mine, cnorm,
           in_sem, s_sw, r_sw, s_row, r_row, s_sib, r_sib, s_rot, r_rot, s_tp, r_tp, s_cz, r_cz, s_cx, r_cx):
    r = lax.axis_index("prow")
    q = lax.axis_index("pcol")
    x = r % 4
    zl = r // 4
    c = q % 2
    oc = 1 - c
    y = (q // 2) % 4
    zh = q // 8
    rc = rows.shape[3]
    half = NC * rc

    def at_q(zhi, yy, cc):
        return {"prow": r, "pcol": zhi * 8 + yy * 2 + cc}

    def at_r(rr):
        return {"prow": rr, "pcol": q}

    sib = at_q(zh, y, oc)
    up = at_q(zh, (y + 1) % 4, c)
    down = at_q(zh, (y + 3) % 4, c)
    across = at_q(1 - zh, y, c)
    flip = {"prow": q, "pcol": r}

    load = pltpu.make_async_copy(x_hbm, xv, in_sem)
    load.start()
    bar = pltpu.get_barrier_semaphore()
    for d in (sib, up, down, across):
        pl.semaphore_signal(bar, inc=1, device_id=d, device_id_type=MESH)
    for d in range(1, 16):
        pl.semaphore_signal(bar, inc=1, device_id=at_r((r + d) % 16), device_id_type=MESH)

    @pl.when(q != r)
    def _():
        pl.semaphore_signal(bar, inc=1, device_id=flip, device_id_type=MESH)

    load.wait()
    off0 = off_ref[0]
    slot = lax.shift_right_logical(off0 - r + 15, 4)
    rot1[0] = pick([xv[:, s * TB:(s + 2) * TB] for s in range(xv.shape[1] // TB - 1)], slot)
    mine[1] = xv[:, xv.shape[1] - 2 * TB:]
    pl.semaphore_wait(bar, 19 + (q != r).astype(jnp.int32))

    def swap(i):
        return pltpu.make_async_remote_copy(
            xv.at[:, pl.ds(pl.multiple_of(oc * half + i * rc, rc), rc)], tr.at[i, c],
            s_sw.at[i], r_sw.at[i], device_id=sib, device_id_type=MESH)

    @pl.loop(0, NC)
    def _(i):
        swap(i).start()

    def turn(stage, d):
        buf = rot1 if stage == 0 else rot2
        step = 1 if stage == 0 else 4
        return pltpu.make_async_remote_copy(
            buf.at[0], buf.at[d], s_rot.at[stage, d - 1], r_rot.at[stage, d - 1],
            device_id=at_r((r + 16 - step * d) % 16), device_id_type=MESH)

    def flipped(p):
        return pltpu.make_async_remote_copy(
            mine.at[p], cols.at[p, zh * 2 + y // 2, (y % 2) * 2 + c], s_tp.at[p], r_tp.at[p],
            device_id=flip, device_id_type=MESH)

    def flip_start(p):
        @pl.when(q != r)
        def _():
            flipped(p).start()

        @pl.when(q == r)
        def _():
            cols[p, zl, x] = mine[p]

    def flip_wait(p):
        @pl.when(q != r)
        def _():
            flipped(p).wait_recv()

    def col_z(p, d):
        return pltpu.make_async_remote_copy(
            cols.at[p, zl, x], cols.at[p, zl, x], s_cz.at[p, d - 1], r_cz.at[p, d - 1],
            device_id=at_r((r + 4 * d) % 16), device_id_type=MESH)

    def col_z_wait(p, d):
        src = cols.at[p, (zl + 4 - d) % 4, x]
        return pltpu.make_async_remote_copy(
            src, src, s_cz.at[p, d - 1], r_cz.at[p, d - 1],
            device_id=at_r((r + 4 * d) % 16), device_id_type=MESH)

    def col_x(p, d):
        return pltpu.make_async_remote_copy(
            cols.at[p, :, x], cols.at[p, :, x], s_cx.at[p, d - 1], r_cx.at[p, d - 1],
            device_id=at_r(zl * 4 + (x + d) % 4), device_id_type=MESH)

    def col_x_wait(p, d):
        src = cols.at[p, :, (x + 4 - d) % 4]
        return pltpu.make_async_remote_copy(
            src, src, s_cx.at[p, d - 1], r_cx.at[p, d - 1],
            device_id=at_r(zl * 4 + (x + d) % 4), device_id_type=MESH)

    if True:
        for d in (1, 2, 3):
            turn(0, d).start()
        flip_start(1)

    UP, DOWN, FUP, ACROSS = 0, 1, 2, 8

    def base(g):
        return (zh if g == 0 else 1 - zh) * 4

    def row_copy(kind, i, block, lo, n, to):
        ref = rows.at[c, i, block, pl.ds(lo, n)]
        return pltpu.make_async_remote_copy(ref, ref, s_row.at[kind, i], r_row.at[kind, i],
                                            device_id=to, device_id_type=MESH)

    def send_up(g, i):
        return row_copy(4 * g + UP, i, base(g) + y, 0, rc, up)

    def send_down(g, i):
        return row_copy(4 * g + DOWN, i, base(g) + y, 0, rc, down)

    def send_across(i):
        return row_copy(ACROSS, i, base(0) + y, 0, rc, across)

    def passing(g, i, each):
        @pl.when((i + g) % 2 == 0)
        def _():
            each(row_copy(4 * g + FUP, i, base(g) + (y + 3) % 4, 0, rc, up))

        @pl.when((i + g) % 2 == 1)
        def _():
            each(row_copy(4 * g + FUP, i, base(g) + (y + 1) % 4, 0, rc, down))

    def pass_on(g, i):
        passing(g, i, lambda copy: copy.start())

    def got_up(g, i):
        return row_copy(4 * g + UP, i, base(g) + (y + 3) % 4, 0, rc, up)

    def got_down(g, i):
        return row_copy(4 * g + DOWN, i, base(g) + (y + 1) % 4, 0, rc, down)

    def got_across(i):
        return row_copy(ACROSS, i, base(1) + y, 0, rc, across)

    def got_passed(g, i):
        return row_copy(4 * g + FUP, i, base(g) + (y + 2) % 4, 0, rc, up)

    def share(g, i, h):
        ref = rows.at[h, i, pl.ds(base(g), 4)]
        return pltpu.make_async_remote_copy(ref, ref, s_sib.at[g, i], r_sib.at[g, i],
                                            device_id=sib, device_id_type=MESH)

    own = zh * 4 + y

    def launch(i):
        tr[i, c] = xv[:, pl.ds(pl.multiple_of(c * half + i * rc, rc), rc)]
        pltpu.make_async_remote_copy(tr.at[i, oc], tr.at[i, oc], s_sw.at[i], r_sw.at[i],
                                     device_id=sib, device_id_type=MESH).wait_recv()
        rows[c, i, own] = tr[i].reshape(2 * tr.shape[2], rc).T
        send_up(0, i).start()
        send_down(0, i).start()

    @pl.loop(0, AHEAD)
    def _(i):
        launch(i)

    if True:
        for d in (1, 2, 3):
            turn(0, d).wait_recv()
        rot2[0] = pick([rot1[d] for d in range(4)], lax.bitwise_and(off0, 3))
        for d in (1, 2, 3):
            turn(1, d).start()

    ls = ls_ref[0]
    var = var_ref[0]
    scale = 5.0 / (ls * ls)

    def norms(p):
        for d in (1, 2, 3):
            col_x_wait(p, d).wait_recv()
        if p == 1:
            cnorm[p] = col_norm(cols, p)

    def compute(i):
        lhs = gathered(rows, i)
        rnorm[i] = jnp.sum(jnp.square(lhs.astype(F32)), axis=1, keepdims=True)
        out = values(lhs, rnorm[i], cols[1], cnorm[1], scale, var)
        for h in (0, 1):
            o_ref[pl.ds(pl.multiple_of(h * half + i * rc, rc), rc), :] = out[h * rc:(h + 1) * rc]

    def own_pass(lo, hi):
        @pl.loop(lo, hi)
        def _(i):
            got_up(0, i).wait_recv()
            got_down(0, i).wait_recv()
            pass_on(0, i)

    @pl.loop(0, ZWIN)
    def _(i):
        send_across(i).start()

    def panel1_z():
        flip_wait(1)
        for d in (1, 2, 3):
            col_z(1, d).start()

    def panel0_flip():
        for d in (1, 2, 3):
            turn(1, d).wait_recv()
        mine[0] = pick([rot2[d] for d in range(4)], lax.bitwise_and(lax.shift_right_logical(off0, 2), 3))
        flip_start(0)

    own_pass(0, OWN[0])
    if EARLY[0] < 0:
        panel1_z()
    if EARLY[1] < 0:
        panel0_flip()
    own_pass(OWN[0], OWN[1])

    @pl.loop(0, NC + LAG[3])
    def _(s):
        @pl.when(s < NC)
        def _():
            got_across(s).wait_recv()
            send_up(1, s).start()
            send_down(1, s).start()

        if True:
            pl.when(s == EARLY[0])(panel1_z)
            pl.when(s == EARLY[1])(panel0_flip)

            @pl.when(s == STEPS[0])
            def _():
                for d in (1, 2, 3):
                    col_z_wait(1, d).wait_recv()
                for d in (1, 2, 3):
                    col_x(1, d).start()

            @pl.when(s == STEPS[1])
            def _():
                flip_wait(0)
                for d in (1, 2, 3):
                    col_z(0, d).start()

            @pl.when(s == STEPS[2])
            def _():
                for d in (1, 2, 3):
                    col_z_wait(0, d).wait_recv()
                for d in (1, 2, 3):
                    col_x(0, d).start()

        @pl.when(s + ZWIN < NC)
        def _():
            send_across(s + ZWIN).start()

        for k in range(2, len(OWN)):
            @pl.when(s == k - 2)
            def _():
                own_pass(OWN[k - 1], OWN[k])

        b = s - LAG[0]

        @pl.when((b >= 0) & (b < NC))
        def _():
            got_up(1, b).wait_recv()
            got_down(1, b).wait_recv()
            pass_on(1, b)

        e = s - LAG[1]

        @pl.when((e >= 0) & (e < NC))
        def _():
            got_passed(0, e).wait_recv()
            share(0, e, c).start()

        f = s - LAG[2]

        @pl.when((f >= 0) & (f < NC))
        def _():
            got_passed(1, f).wait_recv()
            share(1, f, c).start()

        @pl.when(s == CS1)
        def _():
            norms(1)

        for k in (0, 1):
            g = jnp.where(s < 2 * CS1 - LAG[3], 2 * (s - CS1) + k, s - LAG[3] if k == 0 else -1)

            @pl.when((g >= 0) & (s >= CS1))
            def _():
                share(0, g, oc).wait_recv()
                share(1, g, oc).wait_recv()
                compute(g)

    norms(0)

    if True:
        for stage in (0, 1):
            for d in (1, 2, 3):
                turn(stage, d).wait_send()
        for p in (0, 1):
            @pl.when(q != r)
            def _():
                flipped(p).wait_send()

            for d in (1, 2, 3):
                col_z(p, d).wait_send()
                col_x(p, d).wait_send()

    @pl.loop(0, NC)
    def _(i):
        swap(i).wait_send()
        send_across(i).wait_send()
        for g in (0, 1):
            send_up(g, i).wait_send()
            send_down(g, i).wait_send()
            passing(g, i, lambda copy: copy.wait_send())
            share(g, i, c).wait_send()


def on_device(features, panel_offsets, length_scale, variance):
    pts, width = features.shape
    rc = pts // (2 * NC)
    smem = pl.BlockSpec(memory_space=pltpu.SMEM)
    dma = pltpu.SemaphoreType.DMA
    vmem = pl.BlockSpec(memory_space=pltpu.VMEM)
    first, rows, cols, rnorm = pl.pallas_call(
        kernel,
        out_shape=[
            pltpu.VMEM((pts, 2 * TB), F32),
            pltpu.VMEM((2, NC, 8, rc, 2 * width), BF16),
            pltpu.VMEM((2, 4, 4, width, 2 * TB), BF16),
            pltpu.VMEM((NC, 2 * rc, 1), F32),
        ],
        in_specs=[smem, smem, smem, pl.BlockSpec(memory_space=pl.ANY)],
        out_specs=[vmem] * 4,
        scratch_shapes=[
            pltpu.VMEM((width, pts), BF16),
            pltpu.VMEM((NC, 2, width, rc), BF16),
            pltpu.VMEM((4, width, 2 * TB), BF16),
            pltpu.VMEM((4, width, 2 * TB), BF16),
            pltpu.VMEM((2, width, 2 * TB), BF16),
            pltpu.VMEM((2, 1, 2 * TB), F32),
            dma, dma((NC,)), dma((NC,)), dma((9, NC)), dma((9, NC)), dma((2, NC)), dma((2, NC)),
            dma((2, 3)), dma((2, 3)), dma((2,)), dma((2,)), dma((2, 3)), dma((2, 3)), dma((2, 3)), dma((2, 3)),
        ],
        compiler_params=pltpu.CompilerParams(
            collective_id=0, has_side_effects=True, vmem_limit_bytes=40 * 2**20),
        cost_estimate=pl.CostEstimate(flops=2 * pts * 1024 * 512, bytes_accessed=9 * 2**20, transcendentals=0),
        name="panels",
    )(panel_offsets, length_scale, variance, features.T)
    return pl.pallas_call(
        finish,
        out_shape=jax.ShapeDtypeStruct((2, pts, 2 * TB), F32),
        in_specs=[smem, smem, vmem, vmem, vmem, vmem],
        out_specs=pl.BlockSpec(memory_space=pl.ANY),
        scratch_shapes=[pltpu.VMEM((pts, 2 * TB), F32), dma, dma((NC, 2))],
        compiler_params=pltpu.CompilerParams(vmem_limit_bytes=24 * 2**20),
        name="finish",
    )(length_scale, variance, first, rows, cols, rnorm)


def solution(mesh):
    return jax.shard_map(
        on_device,
        mesh=mesh,
        in_specs=(P("prow", "pcol"), P(), P(), P()),
        out_specs=P(None, "prow", "pcol"),
        check_vma=False,
    )
```

time: 88 us -> 71.4 us (0.81)
  Pallas kernels: 83.2 us -> 69.1 us
  local copies, waits for them, and re-layouts: 3.4 us -> 0 us
    pallas_call x1 -> x2, Pallas kernels: 83.2 us -> 69.1 us  [the longest x1 63.7 us: on_device(): pl.pallas_call(kernel, out_shape=[pltpu.VMEM((pts, 2 * TB), F32), pltpu.V...]
    unnamed x1 -> x0, local copies, waits for them, and re-layouts: 3.4 us -> none
where the time goes in v2:
time: 71.4 us; the launch traced here: 70.5 us
  Pallas kernels  69.1 us (97%)
  between operations  1.31 us (2%)
    pallas_call x1, Pallas kernels, on_device(): pl.pallas_call(kernel, out_shape=[pltpu.VMEM((pts, 2 * TB), F32), pltpu.V...  63.7 us
    pallas_call x1, Pallas kernels, on_device(): pl.pallas_call(finish, out_shape=jax.ShapeDtypeStruct((2, pts, 2 * TB), F...  5.46 us

profile of v2, /device:TPU:1, one launch (start us, length us, event | category | flops | bytes accessed | tf_op | source)
XLA Modules:
  0.0 70.5 jit_solution(4707251844649480367)
XLA Ops:
  1.3 63.7 %panels.1 = (f32[4096,256]{1,0:T(8,128)S(1)}, bf16[2,8,8,256,128]{4,3,2,1,0:T(8,128)(2,1)S(1)}, bf16[2,4,4,64,256]{4,3,2,1,0:T(8,128)(2,1)S(1)}, f32[8,512,1]{2,1,0:T(8,128)S(1)}) custom-call(s32[2]{0:T(128)} %off_ref.1, f32[1]{0:T(128)S(6)} %copy.5.ls_ref, f32[1]{0:T(128)S(6)} %copy.6.var_ref, bf16[64,4096]{1,0:T(8,128)(2,1)} %bitcast.1), custom_call_target="tpu_custom_call" | custom-call | flops 4294967296 | bytes 9437184 | tf_op jit(solution)/shard_map/panels/pallas_call | solution.py:411
  65.0 5.5 %finish.1 = f32[2,4096,256]{2,1,0:T(8,128)} custom-call(f32[1]{0:T(128)S(6)} %copy.5.ls_ref, f32[1]{0:T(128)S(6)} %copy.6.var_ref, f32[4096,256]{1,0:T(8,128)S(1)} %get-tuple-element.9.first, bf16[2,8,8,256,128]{4,3,2,1,0:T(8,128)(2,1)S(1)} %get-tuple-element.10.rows, bf16[2,4,4,64,256]{4,3,2,1,0:T(8,128)(2,1)S(1)} %get-tuple-element.11.cols, ...), custom_call_target="tpu_custom_call" | custom-call | tf_op jit(solution)/shard_map/finish/pallas_call | solution.py:436

commit v3 on v2

--- a/solution.py
+++ b/solution.py
@@ -14,8 +14,8 @@
 ZWIN = 3
 EARLY = (-1, 0)
 OWN = (3, 3, 6, 8)
-STEPS = (2, 4, 7)
-CS1 = 7
+STEPS = (1, 3, 6)
+CS1 = 6
 LOG2E = 1.4426950408889634
 MESH = pl.DeviceIdType.MESH
 BF16 = jnp.bfloat16
@@ -45,7 +45,7 @@
 
 def values(lhs, rn, columns, cn, scale, var):
     gram = jnp.dot(lhs, columns.reshape(lhs.shape[1], 2 * TB), preferred_element_type=F32)
-    sq = jnp.maximum((rn + cn - 2.0 * gram) * scale, 1e-30)
+    sq = jnp.maximum((rn * scale + cn * scale) - (2.0 * scale) * gram, 1e-30)
     dist = sq * lax.rsqrt(sq)
     return (var * (1.0 + dist + sq * (1.0 / 3.0))) * jnp.exp2(dist * (-LOG2E))
 
@@ -64,12 +64,14 @@
         at = pl.ds(pl.multiple_of(h * half + i * rc, rc), rc)
         return pltpu.make_async_copy(stage.at[at], o_hbm.at[0, at], sem0.at[i, h])
 
-    @pl.loop(0, NC)
-    def _(i):
-        out = values(gathered(rows, i), rnorm[i], cols[0], cn, scale, var)
-        for h in (0, 1):
-            stage[pl.ds(pl.multiple_of(h * half + i * rc, rc), rc), :] = out[h * rc:(h + 1) * rc]
-            out_copy(i, h).start()
+    @pl.loop(0, NC // 4)
+    def _(j):
+        parts = [4 * j + k for k in range(4)]
+        outs = [values(gathered(rows, i), rnorm[i], cols[0], cn, scale, var) for i in parts]
+        for i, out in zip(parts, outs):
+            for h in (0, 1):
+                stage[pl.ds(pl.multiple_of(h * half + i * rc, rc), rc), :] = out[h * rc:(h + 1) * rc]
+                out_copy(i, h).start()
 
     send.wait()
 

time: 71.4 us -> 70.4 us (0.986); the launches traced: 70.5 us -> 70.3 us
  no operation moved by 1% of the time
where the time goes in v3:
time: 70.4 us; the launch traced here: 70.3 us
  Pallas kernels  69 us (98%)
  between operations  1.31 us (2%)
    pallas_call x1, Pallas kernels, on_device(): pl.pallas_call(kernel, out_shape=[pltpu.VMEM((pts, 2 * TB), F32), pltpu.V...  64.2 us
    pallas_call x1, Pallas kernels, on_device(): pl.pallas_call(finish, out_shape=jax.ShapeDtypeStruct((2, pts, 2 * TB), F...  4.81 us

profile of v3, /device:TPU:1, one launch (start us, length us, event | category | flops | bytes accessed | tf_op | source)
XLA Modules:
  0.0 70.3 jit_solution(15603543940027850823)
XLA Ops:
  1.3 64.2 %panels.1 = (f32[4096,256]{1,0:T(8,128)S(1)}, bf16[2,8,8,256,128]{4,3,2,1,0:T(8,128)(2,1)S(1)}, bf16[2,4,4,64,256]{4,3,2,1,0:T(8,128)(2,1)S(1)}, f32[8,512,1]{2,1,0:T(8,128)S(1)}) custom-call(s32[2]{0:T(128)} %off_ref.1, f32[1]{0:T(128)S(6)} %copy.5.ls_ref, f32[1]{0:T(128)S(6)} %copy.6.var_ref, bf16[64,4096]{1,0:T(8,128)(2,1)} %bitcast.1), custom_call_target="tpu_custom_call" | custom-call | flops 4294967296 | bytes 9437184 | tf_op jit(solution)/shard_map/panels/pallas_call | solution.py:413
  65.5 4.8 %finish.1 = f32[2,4096,256]{2,1,0:T(8,128)} custom-call(f32[1]{0:T(128)S(6)} %copy.5.ls_ref, f32[1]{0:T(128)S(6)} %copy.6.var_ref, f32[4096,256]{1,0:T(8,128)S(1)} %get-tuple-element.9.first, bf16[2,8,8,256,128]{4,3,2,1,0:T(8,128)(2,1)S(1)} %get-tuple-element.10.rows, bf16[2,4,4,64,256]{4,3,2,1,0:T(8,128)(2,1)S(1)} %get-tuple-element.11.cols, ...), custom_call_target="tpu_custom_call" | custom-call | tf_op jit(solution)/shard_map/finish/pallas_call | solution.py:438

commit v4 on v3

--- a/solution.py
+++ b/solution.py
@@ -64,9 +64,9 @@
         at = pl.ds(pl.multiple_of(h * half + i * rc, rc), rc)
         return pltpu.make_async_copy(stage.at[at], o_hbm.at[0, at], sem0.at[i, h])
 
-    @pl.loop(0, NC // 4)
+    @pl.loop(0, NC // 8)
     def _(j):
-        parts = [4 * j + k for k in range(4)]
+        parts = [8 * j + k for k in range(8)]
         outs = [values(gathered(rows, i), rnorm[i], cols[0], cn, scale, var) for i in parts]
         for i, out in zip(parts, outs):
             for h in (0, 1):

time: 70.4 us -> 70.2 us (level)
  no operation moved by 1% of the time
where the time goes in v4:
time: 70.2 us; the launch traced here: 70 us
  Pallas kernels  68.7 us (98%)
  between operations  1.31 us (2%)
    pallas_call x1, Pallas kernels, on_device(): pl.pallas_call(kernel, out_shape=[pltpu.VMEM((pts, 2 * TB), F32), pltpu.V...  64.2 us
    pallas_call x1, Pallas kernels, on_device(): pl.pallas_call(finish, out_shape=jax.ShapeDtypeStruct((2, pts, 2 * TB), F...  4.53 us

profile of v4, /device:TPU:1, one launch (start us, length us, event | category | flops | bytes accessed | tf_op | source)
XLA Modules:
  0.0 70.0 jit_solution(5037281688257079337)
XLA Ops:
  1.3 64.2 %panels.1 = (f32[4096,256]{1,0:T(8,128)S(1)}, bf16[2,8,8,256,128]{4,3,2,1,0:T(8,128)(2,1)S(1)}, bf16[2,4,4,64,256]{4,3,2,1,0:T(8,128)(2,1)S(1)}, f32[8,512,1]{2,1,0:T(8,128)S(1)}) custom-call(s32[2]{0:T(128)} %off_ref.1, f32[1]{0:T(128)S(6)} %copy.5.ls_ref, f32[1]{0:T(128)S(6)} %copy.6.var_ref, bf16[64,4096]{1,0:T(8,128)(2,1)} %bitcast.1), custom_call_target="tpu_custom_call" | custom-call | flops 4294967296 | bytes 9437184 | tf_op jit(solution)/shard_map/panels/pallas_call | solution.py:413
  65.5 4.5 %finish.1 = f32[2,4096,256]{2,1,0:T(8,128)} custom-call(f32[1]{0:T(128)S(6)} %copy.5.ls_ref, f32[1]{0:T(128)S(6)} %copy.6.var_ref, f32[4096,256]{1,0:T(8,128)S(1)} %get-tuple-element.9.first, bf16[2,8,8,256,128]{4,3,2,1,0:T(8,128)(2,1)S(1)} %get-tuple-element.10.rows, bf16[2,4,4,64,256]{4,3,2,1,0:T(8,128)(2,1)S(1)} %get-tuple-element.11.cols, ...), custom_call_target="tpu_custom_call" | custom-call | tf_op jit(solution)/shard_map/finish/pallas_call | solution.py:438
